TPU v7x, 256 devices: a whole 4x4x8 slice. The times are simulated.
256 devices in a mesh: blk: 128 (over y_hi, x, z, core), fsdp: 2 (over y_lo).
Axes of the slice: x: 4, y: 4 (y_hi: 2, y_lo: 2; y = y_hi * 2 + y_lo), z: 8, core: 2. Of those that a mesh axis runs over, the one named last changes fastest.
Arguments:
- image_features: bfloat16 [65536, 1152], P(('blk', 'fsdp')), may hold values from -6 to 6
- text_features: bfloat16 [65536, 1152], P(('blk', 'fsdp')), may hold values from -6 to 6
- image_head: bfloat16 [1152, 1152], P('fsdp'), may hold values from -0.1875 to 0.1875
- text_head: bfloat16 [1152, 1152], P('fsdp'), may hold values from -0.1875 to 0.1875
- pair_index: int32 [256, 256], P(('blk', 'fsdp')), may hold values from 0 to 255, each once within a row
- logit_scale: float32 [1], replicated, may hold values from 2 to 8
- logit_bias: float32 [1], replicated, may hold values from -1 to 0
Outputs:
- image_head_grad: float32 [1152, 1152], P('fsdp')
- text_head_grad: float32 [1152, 1152], P('fsdp')
Inputs may be any that keep to these rules, and one draw needn't show every extreme that they name: Each row of pair_index names every row 0 to 255 of its block exactly once.
All inputs are finite; a program needn't handle non-finite values.
Results may differ from a plain program's by a relative error of at most 0.004.
Values may be sent and summed in bfloat16 or wider, within the bound.
A program may use at most 128 MiB of HBM per device.

v0:
```python
import jax
import jax.numpy as jnp
from jax import lax
from jax.experimental import pallas as pl
from jax.experimental.pallas import tpu as pltpu
from jax.sharding import PartitionSpec as P

STEPS = 8
MESH = pl.DeviceIdType.MESH
ROWS = 256
E = 1152
HALF = E // 2
SLOTS = 5
EARLY = 512
WIDEN = 2
WIDTHS = (384, 384, 384)
PARTS = len(WIDTHS)
STARTS = tuple(sum(WIDTHS[:n]) for n in range(PARTS))
BITS = 4
RELAY = 0
BIT = ROWS // BITS
DIRECT = 192
SHARE = (HALF - DIRECT) // 4
SHARE_FAR = 64
SHARE_NEAR = SHARE - SHARE_FAR
XROWS = HALF // 4
PIECE = 16
PWIDE = E + 128 * PARTS


def device_of(x, yh, f, z, core):
    return (((yh * 4 + x) * 8 + z) * 2 + core, f)


def shifted(index, by):
    other = lax.rem(index + (by + 256), 256)
    return (lax.div(other, 2), lax.rem(other, 2))


def is_equal(n, k):
    gap = n - k
    return 1 - lax.div(gap * gap + 99, 100)


def kernel(
    image_ref,
    text_ref,
    image_head_ref,
    text_head_ref,
    pair_ref,
    scale_ref,
    bias_ref,
    image_out,
    text_out,
    feats,
    feats_t,
    head,
    raw,
    inv,
    emb,
    emb_other,
    grad,
    raw_grad,
    relay,
    pairs,
    signs,
    y_out,
    y_in,
    total,
    x_out,
    x_in,
    x_sum,
    z_out,
    z_in,
    z_sum,
    y2_in,
    final,
    z_all,
    mine,
    other,
    feat_send,
    feat_recv,
    bit_send,
    bit_recv,
    relay_send,
    relay_recv,
    head_send,
    head_recv,
    pair_send,
    pair_recv,
    emb_send,
    emb_recv,
    y_send,
    y_recv,
    x_send,
    x_recv,
    z_send,
    z_recv,
    y2_send,
    y2_recv,
    zag_send,
    zag_recv,
    xag_send,
    xag_recv,
    core_send,
    core_recv,
    out_sem,
):
    blk = lax.axis_index("blk")
    f = lax.axis_index("fsdp")
    core = lax.rem(blk, 2)
    z = lax.rem(lax.div(blk, 2), 8)
    x = lax.rem(lax.div(blk, 16), 4)
    yh = lax.div(blk, 64)
    index = blk * 2 + f
    sibling = device_of(x, yh, f, z, 1 - core)
    near = device_of(x, yh, 1 - f, z, core)
    far = device_of(x, 1 - yh, 1 - f, z, core)
    across = device_of(x, 1 - yh, f, z, core)
    x_peers = [device_of(lax.rem(x + k, 4), yh, f, z, core) for k in range(1, 4)]
    z_peers = [device_of(x, yh, f, lax.rem(z + k, 8), core) for k in range(1, 8)]
    step = 3 - 2 * lax.rem(core + f, 2)

    barrier = pltpu.get_barrier_semaphore()

    def hello(device):
        pl.semaphore_signal(barrier, inc=1, device_id=device, device_id_type=MESH)

    for device in [sibling, near, far, across] + x_peers + z_peers:
        hello(device)

    @pl.when(core == 0)
    def _():
        hello(shifted(index, 1))
        hello(shifted(index, 3))

    z_last = lax.div(z, 7)
    z_first = (1 - lax.div(z + 6, 7)) * core
    leaves = z_last * (1 - core)
    turns = z_last * lax.div(x, 3) * core * RELAY
    starts = z_first * (1 - lax.div(x + 2, 3)) * RELAY
    ahead = shifted(index, 32)

    @pl.when(core == 1)
    def _():
        hello(shifted(index, -4))

        @pl.when(z_first == 0)
        def _():
            hello(shifted(index, -6))

        @pl.when(z_first == 1)
        def _():
            hello(device_of(x, yh, f, 7, 0))

    @pl.when(starts == 1)
    def _():
        hello(device_of(3, yh, f, 7, 1))

    @pl.when(leaves == 1)
    def _():
        hello(shifted(index, -32))

    def rows_of(ref, slot):
        start = slot * ROWS
        if not isinstance(slot, int):
            start = pl.multiple_of(start, ROWS)
        return ref.at[pl.ds(start, ROWS)]

    def remote(src, dst, send, recv, device):
        return pltpu.make_async_remote_copy(
            src_ref=src, dst_ref=dst, send_sem=send, recv_sem=recv,
            device_id=device, device_id_type=MESH,
        )

    def feat_copy(src, slot, which, device):
        return remote(src, rows_of(feats, slot), feat_send.at[which], feat_recv.at[slot], device)

    own_half = pl.multiple_of(f * HALF, 16)
    own_pair = pltpu.make_async_copy(pair_ref, pairs.at[0], pair_send.at[0])
    own_pair.start()

    @pl.when(core == 0)
    def _():
        pltpu.make_async_copy(image_ref, rows_of(feats, 0), feat_recv.at[0]).start()
        pltpu.make_async_copy(image_head_ref, head.at[pl.ds(own_half, HALF)], head_recv.at[0]).start()

    @pl.when(core == 1)
    def _():
        pltpu.make_async_copy(text_ref, rows_of(feats, 0), feat_recv.at[0]).start()
        pltpu.make_async_copy(text_head_ref, head.at[pl.ds(own_half, HALF)], head_recv.at[0]).start()

    pl.semaphore_wait(barrier, 16 + leaves + turns)

    def half_rows(half, start, size):
        return pl.ds(pl.multiple_of(half * HALF + start, 16), size)

    def head_copy(src, n, start, size, device):
        return remote(src.at[pl.ds(pl.multiple_of(start, 16), size)], head.at[half_rows(f, start, size)],
                      head_send.at[n], head_recv.at[n + 1], device)

    def head_copies(src):
        return (
            head_copy(src, 1, DIRECT + SHARE * x, SHARE_FAR, far),
            head_copy(src, 2, DIRECT + SHARE * x + SHARE_FAR, SHARE_NEAR, near),
            head_copy(src, 0, 0, DIRECT, far),
        )

    def share_rows(owner, n):
        start = DIRECT + SHARE * owner + n * SHARE_FAR
        return half_rows(1 - f, start, (SHARE_FAR, SHARE_NEAR)[n])

    def share_copy(n, k):
        rows = share_rows(x, n)
        return remote(head.at[rows], head.at[rows], head_send.at[3 + 3 * n + k - 1],
                      head_recv.at[4 + 3 * n + k - 1], x_peers[k - 1])

    pair_copy = remote(pair_ref, pairs.at[1], pair_send.at[1], pair_recv, sibling)

    def bit_copy(src, src_slot, n, slot, device):
        start = slot * ROWS + n * BIT
        return remote(src.at[pl.ds(src_slot * ROWS + n * BIT, BIT)], feats.at[pl.ds(start, BIT)],
                      bit_send.at[slot // 4, n], bit_recv.at[slot - 2, n], device)

    def relay_in(src, n, device):
        rows = pl.ds(n * BIT, BIT)
        return remote(src.at[rows], relay.at[rows], bit_send.at[0, n], relay_recv.at[n], device)

    def relay_on(n, slot, device):
        return remote(relay.at[pl.ds(n * BIT, BIT)], feats.at[pl.ds(slot * ROWS + n * BIT, BIT)],
                      relay_send.at[n], bit_recv.at[slot - 2, n], device)

    def bit_wait(slot, n):
        bit_copy(feats, slot, n, slot, across).wait_recv()

    @pl.when(core == 0)
    def _():


        @pl.when(leaves == 0)
        def _():
            for n in range(BITS):
                bit_copy(text_ref, 0, n, 3, shifted(index, 6)).start()

        @pl.when(leaves == 1)
        def _():
            for n in range(BITS):
                relay_in(text_ref, n, ahead).start()

        for copy in head_copies(image_head_ref):
            copy.start()
        feat_copy(image_ref, step, 0, shifted(index, -step)).start()
        feat_copy(text_ref, 1, 1, sibling).start()

    @pl.when(core == 1)
    def _():

        @pl.when(turns == 0)
        def _():
            for n in range(BITS):
                bit_copy(text_ref, 0, n, 2, shifted(index, 4)).start()

        @pl.when(turns == 1)
        def _():
            for n in range(BITS):
                relay_in(text_ref, n, across).start()

        for copy in head_copies(text_head_ref):
            copy.start()
        feat_copy(image_ref, step, 0, shifted(index, -step)).start()
        feat_copy(image_ref, 2, 1, sibling).start()

    pair_copy.start()

    grad[...] = jnp.zeros_like(grad)

    @pl.when(core == 0)
    def _():
        rows_of(feats, 4)[...] = jnp.zeros((ROWS, E), jnp.bfloat16)
        rows_of(raw_grad, 4)[...] = jnp.zeros((ROWS, E), jnp.bfloat16)

    own_pair.wait()
    pair_copy.wait()
    signs[2] = jnp.ones((ROWS, ROWS), jnp.float32)
    for which in range(2):
        hit = lax.broadcasted_iota(jnp.int32, (ROWS, ROWS), 0) == pairs[which]
        sign = jnp.where(hit, -1.0, 1.0).astype(jnp.float32)

        @pl.when(core == 0)
        def _():
            signs[which] = sign.T

        @pl.when(core == 1)
        def _():
            signs[1 - which] = sign

    def feat_wait(slot):
        pltpu.make_async_copy(rows_of(feats, slot), rows_of(feats, slot), feat_recv.at[slot]).wait()

    def turn(slot):
        feats_t[:, slot * ROWS : (slot + 1) * ROWS] = rows_of(feats, slot)[...].T

    def head_wait(rows, sem):
        pltpu.make_async_copy(head.at[rows], head.at[rows], head_recv.at[sem]).wait()

    other_half = pl.multiple_of((1 - f) * HALF, 16)

    for n in range(2):
        head_wait(share_rows(x, n), 2 + n)
        for k in range(1, 4):
            share_copy(n, k).start()

    for n in range(BITS):
        @pl.when(leaves == 1)
        def _():
            relay_in(text_ref, n, ahead).wait_recv()
            relay_on(n, 3, device_of(x, yh, f, 0, 1)).start()

        @pl.when(turns == 1)
        def _():
            relay_in(text_ref, n, across).wait_recv()
            relay_on(n, 2, device_of(0, yh, f, 0, 1)).start()

        @pl.when(core == 1)
        def _():
            bit_wait(2, n)
            bit_copy(feats, 2, n, 4, shifted(index, 4)).start()

    @pl.when(core == 0)
    def _():
        feat_wait(2)

    for slot in (0, 1):
        feat_wait(slot)

    head_wait(pl.ds(own_half, HALF), 0)
    early = pl.ds(pl.multiple_of(f * (E - EARLY), 128), EARLY)
    late = pl.ds(pl.multiple_of((1 - f) * EARLY, 128), E - EARLY)

    def begin(slot, carry):
        rows_of(raw, slot)[...] = jnp.dot(
            rows_of(feats, slot)[:, early], head[early, :], preferred_element_type=jnp.float32
        )
        return carry

    lax.fori_loop(0, 3, begin, 0)
    for slot in (0, 1, 2):
        turn(slot)

    head_wait(half_rows(1 - f, 0, DIRECT), 1)
    for n in range(2):
        for k in range(1, 4):
            head_wait(share_rows(lax.rem(x + 4 - k, 4), n), 4 + 3 * n + k - 1)

    def emb_copy(slot):
        return remote(rows_of(emb, slot), rows_of(emb_other, slot),
                      emb_send.at[slot], emb_recv.at[slot], sibling)

    def embed(slot):
        product = rows_of(raw, slot)[...] + jnp.dot(
            rows_of(feats, slot)[:, late], head[late, :], preferred_element_type=jnp.float32
        )
        inverse = lax.rsqrt(jnp.sum(product * product, axis=1, keepdims=True) + 1e-06)
        unit = product * inverse
        rows_of(raw, slot)[...] = unit
        rows_of(inv, slot)[...] = inverse
        rows_of(emb, slot)[...] = unit.astype(jnp.bfloat16)
        emb_copy(slot).start()

    def embed_step(slot, carry):
        @pl.when((slot == 3) & (core == 0))
        def _():
            feat_wait(3)

        @pl.when((slot == 3) & (core == 1))
        def _():
            for n in range(BITS):
                bit_wait(3, n)

        @pl.when(slot == 3)
        def _():
            begin(3, 0)

        embed(slot)
        return carry

    lax.fori_loop(0, 4, embed_step, 0)

    @pl.when(core == 1)
    def _():
        for n in range(BITS):
            bit_wait(4, n)
        begin(4, 0)
        embed(4)

    turn(3)
    turn(4)

    for slot in range(4):
        @pl.when(core == 0)
        def _():
            emb_copy(slot).wait_recv()

        @pl.when(core == 1)
        def _():
            emb_copy(slot).wait_recv()

    @pl.when(core == 0)
    def _():
        emb_copy(4).wait_recv()

    scale = scale_ref[0]
    bias = bias_ref[0]

    def item(n, carry):
        at0 = lax.div(n, 2)
        at1 = lax.div(n + 1, 2)
        col0 = 1 - lax.div(at0, 2) + 2 * lax.rem(n, 2)
        col1 = 2 * lax.rem(n + 1, 2)
        at = at0 + core * (at1 - at0)
        col = col0 + core * (col1 - col0)
        kind = 2 - (
            is_equal(n, 0) * (2 - core) + is_equal(n, 4) * (1 - core) + is_equal(n, 1) * 2 * core
        )
        block = emb_other[pl.ds(pl.multiple_of(col * ROWS, ROWS), 2 * ROWS)]
        scores = scale * lax.dot_general(
            rows_of(emb, at)[...], block, (((1,), (1,)), ((), ())),
            preferred_element_type=jnp.float32,
        ) + bias
        sign = signs[kind]
        first = sign * (0.0625 + 0.0625 * jnp.tanh((0.5 * sign) * scores[:, :ROWS]))
        second = 0.0625 + 0.0625 * jnp.tanh(0.5 * scores[:, ROWS:])
        slope = jnp.concatenate([first, second], axis=1).astype(jnp.bfloat16)
        here = rows_of(grad, at)
        here[...] += jnp.dot(slope, block, preferred_element_type=jnp.float32)
        return carry

    lax.fori_loop(0, 8, item, 0)

    def finish(slot, carry):
        unit = rows_of(raw, slot)[...]
        slope = scale * rows_of(grad, slot)[...]
        inner = jnp.sum(unit * slope, axis=1, keepdims=True)
        rows_of(raw_grad, slot)[...] = (
            (slope - unit * inner) * rows_of(inv, slot)[...]
        ).astype(jnp.bfloat16)
        return carry

    lax.fori_loop(0, 4, finish, 0)

    @pl.when(core == 1)
    def _():
        finish(4, 0)

    SIDE = HALF // 2

    def cols_of(j):
        return pl.ds(STARTS[j], WIDTHS[j])

    def wide_of(j):
        return pl.ds(STARTS[j] + 128 * j, WIDTHS[j] + 128)

    def main_of(j):
        return pl.ds(STARTS[j] + 128 * j, WIDTHS[j])

    def rest_of(j):
        return pl.ds(STARTS[j] + 128 * j + WIDTHS[j], 128)

    def y_copies(j):
        cols = cols_of(j)
        return (
            remote(y_out.at[pl.ds(0, SIDE), cols], y_in.at[pl.ds(0, SIDE), cols],
                   y_send.at[j, 0], y_recv.at[j, 0], near),
            remote(y_out.at[pl.ds(SIDE, SIDE), cols], y_in.at[pl.ds(SIDE, SIDE), cols],
                   y_send.at[j, 1], y_recv.at[j, 1], far),
        )

    for j in range(PARTS):
        cols = cols_of(j)
        y_out[:, cols] = jnp.dot(
            feats_t[pl.ds(other_half, HALF), :], raw_grad[:, cols], preferred_element_type=jnp.float32
        ).astype(jnp.bfloat16)
        for copy in y_copies(j):
            copy.start()
    for j in range(PARTS):
        cols = cols_of(j)
        total[:, cols] = jnp.dot(
            feats_t[pl.ds(own_half, HALF), :], raw_grad[:, cols], preferred_element_type=jnp.float32
        )

    def x_copy(j, k):
        cols = cols_of(j)
        return remote(x_out.at[k - 1, :, cols], x_in.at[k - 1, :, cols],
                      x_send.at[j, k - 1], x_recv.at[j, k - 1], x_peers[k - 1])

    def z_copy(j, k):
        cols = wide_of(j)
        return remote(z_out.at[k - 1, :, cols], z_in.at[k - 1, :, cols],
                      z_send.at[j, k - 1], z_recv.at[j, k - 1], z_peers[k - 1])

    def y2_copy(j):
        cols = wide_of(j)
        return remote(z_sum.at[:, cols], y2_in.at[:, cols], y2_send.at[j], y2_recv.at[j], across)

    def zag_copy(j, k):
        cols = wide_of(j)
        return remote(final.at[:, cols], z_all.at[k - 1, :, cols],
                      zag_send.at[j, k - 1], zag_recv.at[j, k - 1], z_peers[k - 1])

    def x_rows(at):
        return pl.ds(pl.multiple_of(at * XROWS, 16), XROWS)

    def xag_copy(j, k, at):
        rows, cols = x_rows(at), cols_of(j)
        return remote(mine.at[rows, cols], mine.at[rows, cols],
                      xag_send.at[j, k - 1], xag_recv.at[j, k - 1], x_peers[k - 1])

    def core_copy(j):
        cols = cols_of(j)
        return remote(mine.at[:, cols], other.at[:, cols], core_send.at[j], core_recv.at[j], sibling)

    def stage_a(j):
        cols = cols_of(j)
        for copy in y_copies(j):
            copy.wait_recv()
        for k in range(1, 4):
            rows = x_rows(lax.rem(x + k, 4))
            x_out[k - 1, :, cols] = (
                total[rows, cols] + y_in[rows, cols].astype(jnp.float32)
            ).astype(jnp.bfloat16)
            x_copy(j, k).start()
        x_sum[:, cols] = total[x_rows(x), cols] + y_in[x_rows(x), cols].astype(jnp.float32)

    def extra_cols(j, at):
        block = lax.div(at * (WIDTHS[j] // 128), 8)
        return pl.ds(pl.multiple_of(STARTS[j] + block * 128, 128), 128)

    def piece_rows(at):
        return pl.ds(pl.multiple_of(at * PIECE, PIECE), PIECE)

    def stage_b(j):
        cols = cols_of(j)
        for k in range(1, 4):
            x_copy(j, k).wait_recv()
        x_sum[:, cols] = (
            x_sum[:, cols] + x_in[0, :, cols].astype(jnp.float32)
        ) + (x_in[1, :, cols].astype(jnp.float32) + x_in[2, :, cols].astype(jnp.float32))
        for k in range(1, 8):
            at = lax.rem(z + k, 8)
            z_out[k - 1, :, main_of(j)] = x_sum[piece_rows(at), cols].astype(jnp.bfloat16)
            z_out[k - 1, :, rest_of(j)] = x_sum[8 * PIECE :, extra_cols(j, at)].astype(jnp.bfloat16)
            z_copy(j, k).start()
        z_sum[:, main_of(j)] = x_sum[piece_rows(z), cols]
        z_sum[:, rest_of(j)] = x_sum[8 * PIECE :, extra_cols(j, z)]

    def stage_c(j):
        cols = wide_of(j)
        for k in range(1, 8):
            z_copy(j, k).wait_recv()
        acc = z_sum[:, cols]
        for k in range(1, 8):
            acc = acc + z_in[k - 1, :, cols].astype(jnp.float32)
        z_sum[:, cols] = acc
        y2_copy(j).start()

    def place(j, at, piece):
        rows = pl.ds(pl.multiple_of(x * XROWS + at * PIECE, PIECE), PIECE)
        mine[rows, cols_of(j)] = piece[:, : WIDTHS[j]]
        tail = pl.ds(pl.multiple_of(x * XROWS + 8 * PIECE, PIECE), PIECE)
        blocks = WIDTHS[j] // 128
        for n in range(blocks):
            @pl.when(at == -(-8 * n // blocks))
            def _():
                mine[tail, pl.ds(STARTS[j] + n * 128, 128)] = piece[:, WIDTHS[j] :]

    def stage_d(j):
        cols = wide_of(j)
        y2_copy(j).wait_recv()
        final[:, cols] = (z_sum[:, cols] + y2_in[:, cols]).astype(jnp.bfloat16)
        for k in range(1, 8):
            zag_copy(j, k).start()
        place(j, z, final[:, cols])

    def stage_e(j):
        for k in range(1, 8):
            zag_copy(j, k).wait_recv()
            place(j, lax.rem(z + 8 - k, 8), z_all[k - 1, :, wide_of(j)])
        for k in range(1, 4):
            xag_copy(j, k, x).start()

    def stage_f(j):
        for k in range(1, 4):
            xag_copy(j, k, lax.rem(x + 4 - k, 4)).wait_recv()
        core_copy(j).start()

    def out_copies(j, first, second):
        cols = cols_of(j)
        return (
            pltpu.make_async_copy(mine.at[:, cols], first.at[:, cols], out_sem.at[j, 0]),
            pltpu.make_async_copy(other.at[:, cols], second.at[:, cols], out_sem.at[j, 1]),
        )

    def stage_g(j):
        core_copy(j).wait_recv()

        @pl.when(core == 0)
        def _():
            for copy in out_copies(j, image_out, text_out):
                copy.start()

        @pl.when(core == 1)
        def _():
            for copy in out_copies(j, text_out, image_out):
                copy.start()

    stages = (stage_a, stage_b, stage_c, stage_d, stage_e, stage_f, stage_g)
    for turn_at in range(len(stages) + PARTS - 1):
        for j in range(PARTS):
            if 0 <= turn_at - j < len(stages):
                stages[turn_at - j](j)

    for copy in head_copies(image_head_ref):
        copy.wait_send()
    for n in range(2):
        for k in range(1, 4):
            share_copy(n, k).wait_send()

    for which in range(2):
        feat_copy(image_ref, 0, which, sibling).wait_send()
    for n in range(BITS):
        bit_copy(text_ref, 0, n, 2, across).wait_send()

    @pl.when(core == 1)
    def _():
        for n in range(BITS):
            bit_copy(feats, 2, n, 4, across).wait_send()
        emb_copy(4).wait_send()

    @pl.when(leaves + turns == 1)
    def _():
        for n in range(BITS):
            relay_on(n, 2, across).wait_send()

    for slot in range(4):
        emb_copy(slot).wait_send()
    for j in range(PARTS):
        for copy in y_copies(j):
            copy.wait_send()
        for k in range(1, 4):
            x_copy(j, k).wait_send()
            xag_copy(j, k, x).wait_send()
        for k in range(1, 8):
            z_copy(j, k).wait_send()
            zag_copy(j, k).wait_send()
        y2_copy(j).wait_send()
        core_copy(j).wait_send()
        for copy in out_copies(j, image_out, text_out):
            copy.wait()


def widen(image_ref, text_ref, image_out, text_out):
    image_out[...] = image_ref[...].astype(jnp.float32)
    text_out[...] = text_ref[...].astype(jnp.float32)


def on_device(
    image_features, text_features, image_head, text_head, pair_index, logit_scale, logit_bias
):
    hbm = pl.BlockSpec(memory_space=pl.ANY)
    smem = pl.BlockSpec(memory_space=pltpu.SMEM)
    bf16, f32 = jnp.bfloat16, jnp.float32
    vmem = pltpu.VMEM
    dma = pltpu.SemaphoreType.DMA
    image_half, text_half = pl.pallas_call(
        kernel,
        out_shape=(
            jax.ShapeDtypeStruct((HALF, E), bf16),
            jax.ShapeDtypeStruct((HALF, E), bf16),
        ),
        in_specs=[hbm, hbm, hbm, hbm, hbm, smem, smem],
        out_specs=(hbm, hbm),
        scratch_shapes=[
            vmem((SLOTS * ROWS, E), bf16),
            vmem((E, SLOTS * ROWS), bf16),
            vmem((E, E), bf16),
            vmem((SLOTS * ROWS, E), f32),
            vmem((SLOTS * ROWS, 1), f32),
            vmem((SLOTS * ROWS, E), bf16),
            vmem((SLOTS * ROWS, E), bf16),
            vmem((SLOTS * ROWS, E), f32),
            vmem((SLOTS * ROWS, E), bf16),
            vmem((ROWS, E), bf16),
            vmem((2, 1, ROWS), jnp.int32),
            vmem((3, ROWS, ROWS), f32),
            vmem((HALF, E), bf16),
            vmem((HALF, E), bf16),
            vmem((HALF, E), f32),
            vmem((3, XROWS, E), bf16),
            vmem((3, XROWS, E), bf16),
            vmem((XROWS, E), f32),
            vmem((7, PIECE, PWIDE), bf16),
            vmem((7, PIECE, PWIDE), bf16),
            vmem((PIECE, PWIDE), f32),
            vmem((PIECE, PWIDE), f32),
            vmem((PIECE, PWIDE), bf16),
            vmem((7, PIECE, PWIDE), bf16),
            vmem((HALF, E), bf16),
            vmem((HALF, E), bf16),
            dma((2,)),
            dma((SLOTS,)),
            dma((2, BITS)),
            dma((3, BITS)),
            dma((BITS,)),
            dma((BITS,)),
            dma((9,)),
            dma((10,)),
            dma((2,)),
            dma,
            dma((SLOTS,)),
            dma((SLOTS,)),
            dma((PARTS, 2)),
            dma((PARTS, 2)),
            dma((PARTS, 3)),
            dma((PARTS, 3)),
            dma((PARTS, 7)),
            dma((PARTS, 7)),
            dma((PARTS,)),
            dma((PARTS,)),
            dma((PARTS, 7)),
            dma((PARTS, 7)),
            dma((PARTS, 3)),
            dma((PARTS, 3)),
            dma((PARTS,)),
            dma((PARTS,)),
            dma((PARTS, 2)),
        ],
        compiler_params=pltpu.CompilerParams(
            collective_id=0, has_side_effects=True, vmem_limit_bytes=60 * 2**20
        ),
        cost_estimate=pl.CostEstimate(
            flops=12 * 10**9, bytes_accessed=12 * 10**6, transcendentals=10**6
        ),
    )(image_features, text_features, image_head, text_head, pair_index, logit_scale, logit_bias)
    block = pl.BlockSpec((HALF // WIDEN, E), lambda n: (n, 0))
    return pl.pallas_call(
        widen,
        grid=(WIDEN,),
        out_shape=(
            jax.ShapeDtypeStruct((HALF, E), f32),
            jax.ShapeDtypeStruct((HALF, E), f32),
        ),
        in_specs=[block, block],
        out_specs=(block, block),
        compiler_params=pltpu.CompilerParams(vmem_limit_bytes=40 * 2**20),
        cost_estimate=pl.CostEstimate(flops=2 * HALF * E, bytes_accessed=12 * HALF * E, transcendentals=0),
    )(image_half, text_half)


def solution(mesh):
    placed = (
        P(("blk", "fsdp"), None),
        P(("blk", "fsdp"), None),
        P("fsdp", None),
        P("fsdp", None),
        P(("blk", "fsdp"), None),
        P(),
        P(),
    )
    return jax.shard_map(
        on_device,
        mesh=mesh,
        in_specs=placed,
        out_specs=(P("fsdp", None), P("fsdp", None)),
        check_vma=False,
    )
```

profile of v0, /device:TPU:1, one launch (start us, length us, event | category | flops | bytes accessed | tf_op | source)
XLA Modules:
  0.0 116.2 jit_solution(18043103858042364514)
XLA Ops:
  1.9 109.2 %shard_map.86 = (bf16[576,1152]{1,0:T(8,128)(2,1)}, bf16[576,1152]{1,0:T(8,128)(2,1)}) custom-call(bf16[256,1152]{1,0:T(8,128)(2,1)} %image_ref.1, bf16[256,1152]{1,0:T(8,128)(2,1)} %text_ref.1, bf16[576,1152]{1,0:T(8,128)(2,1)} %image_head_ref.1, bf16[576,1152]{1,0:T(8,128)(2,1)} %text_head_ref.1, s32[1,256]{1,0:T(1,128)} %pair_ref.1, f32[1]{0:T(128)S(6)} %copy.9.scale_ref, ...), custom_call_target="tpu_custom_call" | custom-call | flops 12000000000 | bytes 12000000 | tf_op jit(solution)/shard_map/pallas_call | solution.py:674
  111.1 0.0 copy-start
  111.1 1.3 %copy-done = bf16[576,1152]{1,0:T(8,128)(2,1)S(1)} copy-done((bf16[576,1152]{1,0:T(8,128)(2,1)S(1)}, bf16[576,1152]{1,0:T(8,128)(2,1)}, u32[]{:S(2)}) %copy-start) | copy-done | bytes 1327128
  112.4 0.0 copy-start.1
  112.4 1.3 %copy-done.1 = bf16[576,1152]{1,0:T(8,128)(2,1)S(1)} copy-done((bf16[576,1152]{1,0:T(8,128)(2,1)S(1)}, bf16[576,1152]{1,0:T(8,128)(2,1)}, u32[]{:S(2)}) %copy-start.1) | copy-done | bytes 1327128
  113.8 2.5 %shard_map.87 = (f32[576,1152]{1,0:T(8,128)}, f32[576,1152]{1,0:T(8,128)}) custom-call(bf16[576,1152]{1,0:T(8,128)(2,1)S(1)} %copy-done, bf16[576,1152]{1,0:T(8,128)(2,1)S(1)} %copy-done.1), custom_call_target="tpu_custom_call" | custom-call | flops 1327104 | bytes 7962624 | tf_op jit(solution)/shard_map/pallas_call | solution.py:745
Async XLA Ops:
  111.1 1.3 %copy-start = (bf16[576,1152]{1,0:T(8,128)(2,1)S(1)}, bf16[576,1152]{1,0:T(8,128)(2,1)}, u32[]{:S(2)}) copy-start(bf16[576,1152]{1,0:T(8,128)(2,1)} %get-tuple-element.4.image_ref) | copy-start | bytes 3981316
  112.4 1.3 %copy-start.1 = (bf16[576,1152]{1,0:T(8,128)(2,1)S(1)}, bf16[576,1152]{1,0:T(8,128)(2,1)}, u32[]{:S(2)}) copy-start(bf16[576,1152]{1,0:T(8,128)(2,1)} %get-tuple-element.5.text_ref) | copy-start | bytes 3981316
where the time goes:
time: 116 us
  Pallas kernels  112 us (97%)
  local copies, waits for them, and re-layouts  2.64 us (2%)
  between operations  1.94 us (2%)
    pallas_call x1, Pallas kernels, on_device(): pl.pallas_call(kernel, out_shape=(jax.ShapeDtypeStruct((HALF, E), bf16),...  109 us
    unnamed x4, local copies, waits for them, and re-layouts  2.64 us
    pallas_call x1, Pallas kernels, on_device(): pl.pallas_call(widen, grid=(WIDEN,), out_shape=(jax.ShapeDtypeStruct((HAL...  2.49 us

commit v1 on v0

--- a/solution.py
+++ b/solution.py
@@ -751,7 +751,7 @@
         ),
         in_specs=[block, block],
         out_specs=(block, block),
-        compiler_params=pltpu.CompilerParams(vmem_limit_bytes=40 * 2**20),
+        compiler_params=pltpu.CompilerParams(vmem_limit_bytes=60 * 2**20),
         cost_estimate=pl.CostEstimate(flops=2 * HALF * E, bytes_accessed=12 * HALF * E, transcendentals=0),
     )(image_half, text_half)
 

time: 116 us -> 115 us (level)
  local copies, waits for them, and re-layouts: 2.64 us -> 0 us
    unnamed x4 -> x0, local copies, waits for them, and re-layouts: 2.64 us -> none
    pallas_call x1, Pallas kernels: 2.49 us -> 3.79 us  [on_device(): pl.pallas_call(widen, grid=(WIDEN,), out_shape=(jax.ShapeDtypeStruct((HAL...]
where the time goes in v1:
time: 115 us
  Pallas kernels  113 us (98%)
  between operations  1.93 us (2%)
    pallas_call x1, Pallas kernels, on_device(): pl.pallas_call(kernel, out_shape=(jax.ShapeDtypeStruct((HALF, E), bf16),...  109 us
    pallas_call x1, Pallas kernels, on_device(): pl.pallas_call(widen, grid=(WIDEN,), out_shape=(jax.ShapeDtypeStruct((HAL...  3.79 us

profile of v1, /device:TPU:1, one launch (start us, length us, event | category | flops | bytes accessed | tf_op | source)
XLA Modules:
  0.0 114.9 jit_solution(17909255431466723318)
XLA Ops:
  1.9 109.2 %shard_map.86 = (bf16[576,1152]{1,0:T(8,128)(2,1)}, bf16[576,1152]{1,0:T(8,128)(2,1)}) custom-call(bf16[256,1152]{1,0:T(8,128)(2,1)} %image_ref.1, bf16[256,1152]{1,0:T(8,128)(2,1)} %text_ref.1, bf16[576,1152]{1,0:T(8,128)(2,1)} %image_head_ref.1, bf16[576,1152]{1,0:T(8,128)(2,1)} %text_head_ref.1, s32[1,256]{1,0:T(1,128)} %pair_ref.1, f32[1]{0:T(128)S(6)} %copy.9.scale_ref, ...), custom_call_target="tpu_custom_call" | custom-call | flops 12000000000 | bytes 12000000 | tf_op jit(solution)/shard_map/pallas_call | solution.py:674
  111.1 3.8 %shard_map.87 = (f32[576,1152]{1,0:T(8,128)}, f32[576,1152]{1,0:T(8,128)}) custom-call(bf16[576,1152]{1,0:T(8,128)(2,1)} %get-tuple-element.4.image_ref, bf16[576,1152]{1,0:T(8,128)(2,1)} %get-tuple-element.5.text_ref), custom_call_target="tpu_custom_call" | custom-call | flops 1327104 | bytes 7962624 | tf_op jit(solution)/shard_map/pallas_call | solution.py:745

commit v2 on v1

--- a/solution.py
+++ b/solution.py
@@ -237,6 +237,9 @@
     def _():
 
 
+        for copy in head_copies(image_head_ref):
+            copy.start()
+
         @pl.when(leaves == 0)
         def _():
             for n in range(BITS):
@@ -247,14 +250,15 @@
             for n in range(BITS):
                 relay_in(text_ref, n, ahead).start()
 
-        for copy in head_copies(image_head_ref):
-            copy.start()
         feat_copy(image_ref, step, 0, shifted(index, -step)).start()
         feat_copy(text_ref, 1, 1, sibling).start()
 
     @pl.when(core == 1)
     def _():
 
+        for copy in head_copies(text_head_ref):
+            copy.start()
+
         @pl.when(turns == 0)
         def _():
             for n in range(BITS):
@@ -265,8 +269,6 @@
             for n in range(BITS):
                 relay_in(text_ref, n, across).start()
 
-        for copy in head_copies(text_head_ref):
-            copy.start()
         feat_copy(image_ref, step, 0, shifted(index, -step)).start()
         feat_copy(image_ref, 2, 1, sibling).start()
 

time: 115 us -> 115 us (level)
  no operation moved by 1% of the time
where the time goes in v2:
time: 115 us
  Pallas kernels  113 us (98%)
  between operations  1.93 us (2%)
    pallas_call x1, Pallas kernels, on_device(): pl.pallas_call(kernel, out_shape=(jax.ShapeDtypeStruct((HALF, E), bf16),...  109 us
    pallas_call x1, Pallas kernels, on_device(): pl.pallas_call(widen, grid=(WIDEN,), out_shape=(jax.ShapeDtypeStruct((HAL...  3.79 us

profile of v2, /device:TPU:1, one launch (start us, length us, event | category | flops | bytes accessed | tf_op | source)
XLA Modules:
  0.0 114.9 jit_solution(8190217557582435783)
XLA Ops:
  1.9 109.2 %shard_map.86 = (bf16[576,1152]{1,0:T(8,128)(2,1)}, bf16[576,1152]{1,0:T(8,128)(2,1)}) custom-call(bf16[256,1152]{1,0:T(8,128)(2,1)} %image_ref.1, bf16[256,1152]{1,0:T(8,128)(2,1)} %text_ref.1, bf16[576,1152]{1,0:T(8,128)(2,1)} %image_head_ref.1, bf16[576,1152]{1,0:T(8,128)(2,1)} %text_head_ref.1, s32[1,256]{1,0:T(1,128)} %pair_ref.1, f32[1]{0:T(128)S(6)} %copy.9.scale_ref, ...), custom_call_target="tpu_custom_call" | custom-call | flops 12000000000 | bytes 12000000 | tf_op jit(solution)/shard_map/pallas_call | solution.py:676
  111.1 3.8 %shard_map.87 = (f32[576,1152]{1,0:T(8,128)}, f32[576,1152]{1,0:T(8,128)}) custom-call(bf16[576,1152]{1,0:T(8,128)(2,1)} %get-tuple-element.4.image_ref, bf16[576,1152]{1,0:T(8,128)(2,1)} %get-tuple-element.5.text_ref), custom_call_target="tpu_custom_call" | custom-call | flops 1327104 | bytes 7962624 | tf_op jit(solution)/shard_map/pallas_call | solution.py:747
